TPU v7x, 128 devices: a whole 4x4x4 slice. The times are simulated.
128 devices in a mesh: nodes: 32 (over y, z, core), cores: 4 (over x).
Axes of the slice: x: 4, y: 4, z: 4, core: 2. Of those that a mesh axis runs over, the one named last changes fastest.
Arguments:
- coupling: float32 [98304, 384], P(('nodes', 'cores')), may hold values from -0.4 to 0.4
- onsite: float32 [98304], P(('nodes', 'cores')), may hold values from -3 to 3
- row_slot: int32 [98304], replicated, may hold values from 0 to 98303, as said below
- sub_rows: int32 [192, 1024], replicated, may hold values from 0 to 98303, as said below
- sub_host: int32 [192], replicated, may hold values from 0 to 127, as said below
- branches: int32 [3, 192], replicated, may hold values from 0 to 1
Outputs:
- core_density: float32 [256, 512, 1024], P(('nodes', 'cores'))
- occupation: float32 [3], replicated
Inputs may be any that keep to these rules, and one draw needn't show every extreme that they name: `row_slot`: a permutation of the slots; the device holding slot q is q // 768; rows whose numbers are congruent modulo the number of devices are held by the same device. `sub_rows`: each subgraph's rows are 1024 consecutive row numbers modulo 98304; its core rows (positions 256 to 767) of all subgraphs together cover every row once. `sub_host`: every device hosts one or two subgraphs, half of the devices two.
All inputs are finite; a program needn't handle non-finite values.
Results may differ from a plain program's by a relative error of at most 0.0003.
Values sent between devices are 32-bit elements; how exact they have to be, the bound alone decides.
No kernel may reach another device: no remote copies, remote signals or barrier semaphores. Data moves between devices by JAX's collectives and lax.ppermute only.
A program may use at most 128 MiB of HBM per device.

v0:
```python
import jax
import jax.numpy as jnp
from jax import lax
from jax.sharding import PartitionSpec as P

CORE = 512
HALO = 256
ITERS = 3


decay_length = 256.0
epsilon = 1e-06


def assemble(near_rows, site_energy, reach_cols):
    window_size = near_rows.shape[0]
    padded = jnp.concatenate(
        [
            jnp.zeros((window_size, 1), jnp.float32),
            near_rows,
            jnp.zeros((window_size, window_size - reach_cols), jnp.float32),
        ],
        axis=1,
    )
    skewed = padded.reshape(-1)[: window_size * window_size].reshape(window_size, window_size)
    row_index = lax.broadcasted_iota(jnp.int32, (window_size, window_size), 0)
    col_index = lax.broadcasted_iota(jnp.int32, (window_size, window_size), 1)
    offset = col_index - row_index
    falloff = jnp.exp(-offset.astype(jnp.float32) / decay_length)
    upper_part = jnp.where((offset >= 1) & (offset <= reach_cols), skewed * falloff, 0.0)
    return upper_part + upper_part.T + jnp.diag(site_energy)


def spectral_edge(hamiltonian, site_energy):
    off_diagonal = hamiltonian - jnp.diag(site_energy)
    radius = 2.0 * jnp.sqrt(jnp.sum(off_diagonal * off_diagonal, axis=1) + epsilon)
    return (jnp.max(site_energy + radius), jnp.min(site_energy - radius))


def square_step(matrix, branch):
    square = jnp.dot(
        matrix, matrix, precision=lax.Precision.HIGHEST, preferred_element_type=jnp.float32
    )
    return jnp.where(branch == 0, square, 2.0 * matrix - square)


def core_trace(matrix):
    return jnp.trace(matrix[HALO : HALO + CORE, HALO : HALO + CORE])


def on_device(coupling, onsite, row_slot, sub_rows, sub_host, branches):
    devices = lax.axis_size(("nodes", "cores"))
    device_id = lax.axis_index(("nodes", "cores"))
    total_rows = row_slot.shape[0]
    held_rows, reach_cols = coupling.shape
    window_size = sub_rows.shape[1]
    per_owner = window_size // devices
    sub_count = sub_rows.shape[0]
    sub_ids = jnp.arange(sub_count, dtype=jnp.int32)
    earlier = (sub_host[:, None] == sub_host[None, :]) & (sub_ids[None, :] < sub_ids[:, None])
    host_slot = sub_host * 2 + jnp.sum(earlier, axis=1)
    slot_ids = jnp.arange(2 * devices, dtype=jnp.int32)
    matches = host_slot[None, :] == slot_ids[:, None]
    slot_sub = jnp.sum(jnp.where(matches, sub_ids[None, :], 0), axis=1)
    slot_used = jnp.any(matches, axis=1)
    residues = jnp.arange(devices, dtype=jnp.int32)
    residue_owner = row_slot[:devices] // held_rows
    own_residue = jnp.sum(jnp.where(residue_owner == device_id, residues, 0))
    slot_windows = sub_rows[slot_sub]
    first_pos = jnp.mod(own_residue - slot_windows[:, 0], devices)
    positions = first_pos[:, None] + devices * jnp.arange(per_owner, dtype=jnp.int32)[None, :]
    wanted = jnp.take_along_axis(slot_windows, positions, axis=1)
    local_slot = jnp.mod(row_slot[wanted], held_rows)
    keep_mask = slot_used[:, None]
    outgoing = jnp.where(keep_mask[:, :, None], coupling[local_slot], 0.0).reshape(
        devices, 2, per_owner, reach_cols
    )
    outgoing_diag = jnp.where(keep_mask, onsite[local_slot], 0.0).reshape(devices, 2, per_owner)
    arrived, arrived_diag = (
        lax.all_to_all(outgoing, ("nodes", "cores"), split_axis=0, concat_axis=0, tiled=True),
        lax.all_to_all(outgoing_diag, ("nodes", "cores"), split_axis=0, concat_axis=0, tiled=True),
    )
    hamiltonians = []
    highs = []
    lows = []
    chosen_subs = []
    for slot_index in range(2):
        chosen = slot_sub[2 * device_id + slot_index]
        chosen_subs.append(chosen)
        window_rows = sub_rows[chosen]
        source = residue_owner[jnp.mod(window_rows[0] + residues, devices)]
        gathered = arrived[:, slot_index][source]
        near_rows = jnp.transpose(gathered, (1, 0, 2)).reshape(window_size, reach_cols)
        site_energy = arrived_diag[:, slot_index][source].T.reshape(window_size)
        hamiltonian = assemble(near_rows, site_energy, reach_cols)
        upper_value, lower_value = spectral_edge(hamiltonian, site_energy)
        hamiltonians.append(hamiltonian)
        highs.append(upper_value)
        lows.append(lower_value)
    second_used = slot_used[2 * device_id + 1]
    local_high = jnp.maximum(highs[0], jnp.where(second_used, highs[1], highs[0]))
    local_low = jnp.minimum(lows[0], jnp.where(second_used, lows[1], lows[0]))
    spectrum_top = lax.pmax(local_high, ("nodes", "cores"))
    spectrum_bottom = lax.pmin(local_low, ("nodes", "cores"))
    identity = jnp.eye(window_size, dtype=jnp.float32)
    first_matrix = (spectrum_top * identity - hamiltonians[0]) / (spectrum_top - spectrum_bottom)
    second_matrix = (spectrum_top * identity - hamiltonians[1]) / (spectrum_top - spectrum_bottom)
    totals = []
    for iteration in range(ITERS):
        first_branch = branches[iteration, chosen_subs[0]]
        second_branch = branches[iteration, chosen_subs[1]]
        first_matrix = square_step(first_matrix, first_branch)
        second_matrix = lax.cond(
            second_used,
            lambda matrix: square_step(matrix, second_branch),
            lambda matrix: matrix,
            second_matrix,
        )
        local_value = core_trace(first_matrix) + jnp.where(
            second_used, core_trace(second_matrix), 0.0
        )
        totals.append(lax.psum(local_value, ("nodes", "cores")))
    occupation = jnp.stack(totals) / total_rows
    first_core = first_matrix[HALO : HALO + CORE]
    second_core = jnp.where(second_used, second_matrix[HALO : HALO + CORE], 0.0)
    core_density = jnp.stack([first_core, second_core])
    return (core_density, occupation)


def solution(mesh):
    return jax.shard_map(
        on_device,
        mesh=mesh,
        in_specs=(P(("nodes", "cores"), None), P(("nodes", "cores")), P(), P(), P(), P()),
        out_specs=(P(("nodes", "cores"), None, None), P()),
        check_vma=False,
    )
```

profile of v0, /device:TPU:1, one launch (start us, length us, event | category | flops | bytes accessed | tf_op | source)
XLA Modules:
  0.0 589.9 jit_solution(6622093981315229308)
XLA Ops:
  2.8 1.3 fusion.25
  4.2 2.7 gather_fusion
  8.0 16.6 %gather_fusion.10 = s32[2048]{0:T(1024)S(1)} fusion(s32[256,1024]{1,0:T(8,128)S(1)} %gather_fusion, s32[2048]{0:T(1024)S(1)} %reshape.464), kind=kCustom, calls=%fused_computation.10 | custom fusion | bytes 32768 | tf_op jit(solution)/shard_map/jit(take_along_axis)/gather | solution.py:72
  25.6 11.8 %gather_fusion.1 = s32[2048]{0:T(1024)S(1)} fusion(s32[98304]{0:T(1024)S(1)} %copy-done.3, s32[2048]{0:T(1024)S(1)} %broadcast_clamp_fusion.1), kind=kCustom, calls=%fused_computation.1 | custom fusion | bytes 24576 | tf_op jit(solution)/shard_map/gather | solution.py:73
  38.1 8.6 %gather_fusion.2 = f32[2048]{0:T(1024)S(1)} fusion(f32[768]{0:T(1024)S(1)} %copy-done.2, s32[2048]{0:T(1024)S(1)} %broadcast_clamp_fusion), kind=kCustom, calls=%fused_computation.2 | custom fusion | bytes 24576 | tf_op jit(solution)/shard_map/gather | solution.py:78
  47.8 11.5 %all-to-all-start = ((f32[128,2,8]{2,1,0:T(2,128)}), f32[128,2,8]{2,1,0:T(2,128)S(1)}, u32[]{:S(2)}, u32[]{:S(2)}) async-start(f32[128,2,8]{2,1,0:T(2,128)} %broadcast_select_fusion.1), calls=%async_computation | async-start | bytes 262144 | tf_op jit(solution)/shard_map/all_to_all | solution.py:81
  59.3 8.7 %gather_fusion.5 = f32[2048,384]{1,0:T(8,128)} fusion(f32[768,384]{1,0:T(8,128)S(1)} %copy-done, s32[2048]{0:T(1024)S(1)} %broadcast_clamp_fusion), kind=kCustom, calls=%fused_computation.5 | custom fusion | bytes 6299648 | tf_op jit(solution)/shard_map/gather | solution.py:75
  68.0 3.3 broadcast_select_fusion
  71.3 10.6 %all-to-all-start.1 = ((f32[128,2,8,384]{3,2,1,0:T(8,128)}), f32[128,2,8,384]{3,2,1,0:T(8,128)}, u32[]{:S(2)}, u32[]{:S(2)}) async-start(f32[128,2,8,384]{3,2,1,0:T(8,128)} %broadcast_select_fusion), calls=%async_computation.1 | async-start | bytes 6291456 | tf_op jit(solution)/shard_map/all_to_all | solution.py:80
  86.7 1.3 constant_dynamic-slice_fusion.2
  89.2 1.2 gather_fusion.3
  95.7 27.9 %all-to-all-done.1 = f32[128,2,8,384]{3,2,1,0:T(8,128)} async-done(((f32[128,2,8,384]{3,2,1,0:T(8,128)}), f32[128,2,8,384]{3,2,1,0:T(8,128)}, u32[]{:S(2)}, u32[]{:S(2)}) %all-to-all-start.1) | async-done | bytes 3145760 | tf_op jit(solution)/shard_map/all_to_all | solution.py:80
  123.7 3.3 slice_bitcast_fusion.2
  126.9 1.9 gather_fusion.6
  128.8 1.7 copy.111
  130.6 1.7 broadcast.434
  132.3 5.9 %concatenate.6 = f32[1024,1025]{1,0:T(8,128)} concatenate(f32[1024,1]{1,0:T(8,128)S(1)} %broadcast.433, f32[1024,384]{1,0:T(8,128)S(1)} %bitcast.91, f32[1024,640]{1,0:T(8,128)} %broadcast.434), dimensions={1} | concatenate | bytes 8396800 | tf_op jit(solution)/shard_map/concatenate | solution.py:17
  138.3 9.2 %slice.87 = f32[1025,1024]{1,0:T(8,128)} reshape(f32[1024,1025]{1,0:T(8,128)} %concatenate.6) | data formatting | bytes 8396800 | tf_op jit(solution)/shard_map/slice | solution.py:25
  147.4 4.8 slice.127
  152.2 5.4 copy.130
  157.6 5.0 multiply_select_fusion.1
  162.6 5.4 copy.114
  168.0 5.1 fusion.1
  173.8 1.9 gather_fusion.9
  175.8 1.7 copy.119
  177.5 19.1 %concatenate.7 = f32[1024,1025]{1,0:T(8,128)} concatenate(f32[1024,1]{1,0:T(8,128)S(1)} %broadcast.433, f32[1024,384]{1,0:T(8,128)S(1)} %bitcast.92, f32[1024,640]{1,0:T(8,128)} %broadcast.434), dimensions={1} | concatenate | bytes 8396800 | tf_op jit(solution)/shard_map/concatenate | solution.py:17
  196.6 9.2 %slice.92 = f32[1025,1024]{1,0:T(8,128)} reshape(f32[1024,1025]{1,0:T(8,128)} %concatenate.7) | data formatting | bytes 8396800 | tf_op jit(solution)/shard_map/slice | solution.py:25
  205.8 4.8 slice.130
  210.6 5.4 copy.133
  215.9 5.0 multiply_select_fusion
  221.0 5.3 copy.122
  226.3 6.5 %bitcast_add_fusion = f32[1024,1024]{0,1:T(8,128)} fusion(f32[1024,1024]{1,0:T(8,128)} %copy.122, f32[1024,1024]{0,1:T(8,128)} %copy.133), kind=kLoop, calls=%fused_computation.31 | loop fusion | flops 10485760 | bytes 12582912 | tf_op jit(solution)/shard_map/add | solution.py:31
  232.8 5.4 copy.124
  238.2 2.7 fusion.3
  247.3 62.6 %pmin.7 = f32[]{:T(128)} all-reduce(f32[]{:T(128)S(6)} %min.5), channel_id=1, replica_groups=mesh['nodes'=32,'cores'=4] {'nodes','cores'}, use_global_device_ids=true, to_apply=%region_11.12 | all-reduce | flops 1 | bytes 8 | tf_op jit(solution)/shard_map/pmin | solution.py:104
  309.9 62.6 %pmax.7 = f32[]{:T(128)} all-reduce(f32[]{:T(128)S(6)} %max.5), channel_id=1, replica_groups=mesh['nodes'=32,'cores'=4] {'nodes','cores'}, use_global_device_ids=true, to_apply=%region_8.9 | all-reduce | flops 1 | bytes 8 | tf_op jit(solution)/shard_map/pmax | solution.py:103
  373.8 5.8 fusion.5
  379.8 1.9 fusion.15
  381.7 2.7 conditional.4
  384.4 2.0 fusion.13
  386.3 36.3 %subtract_select_fusion.5 = f32[1024,1024]{1,0:T(8,128)S(1)} fusion(pred[]{:T(512)} %bitcast.6, f32[]{:T(128)S(6)} %sub.76, f32[1024]{0:T(1024)S(1)} %bitcast.102, f32[1024,1024]{1,0:T(8,128)} %copy.114, f32[]{:T(128)} %pmax.7, f32[1024,1024]{0,1:T(8,128)} %copy.130), kind=kOutput, calls=%fused_computation.17 | convolution fusion | flops 12921602048 | bytes 12587017 | tf_op jit(solution)/shard_map/dot_general | solution.py:41
  423.3 14.0 %subtract_select_fusion.4 = f32[1024,1024]{1,0:T(8,128)S(1)} fusion(f32[1024,1024]{1,0:T(8,128)S(1)} %subtract_select_fusion.5, pred[]{:T(512)} %bitcast.5), kind=kOutput, calls=%fused_computation.16 | convolution fusion | flops 12888047616 | bytes 8388609 | tf_op jit(solution)/shard_map/dot_general | solution.py:41
  438.0 14.2 %subtract_select_fusion.3 = f32[1024,1024]{1,0:T(8,128)S(1)} fusion(f32[1024,1024]{1,0:T(8,128)S(1)} %subtract_select_fusion.4, pred[]{:T(512)} %bitcast.4), kind=kOutput, calls=%fused_computation.15 | convolution fusion | flops 12888047616 | bytes 8388609 | tf_op jit(solution)/shard_map/dot_general | solution.py:41
  453.1 2.0 fusion.11
  455.1 3.9 fusion.9
  464.8 4.0 pad_maximum_fusion
  468.8 118.3 %all-reduce = (f32[1]{0:T(128)}, f32[1]{0:T(128)}, f32[1]{0:T(128)}) all-reduce(f32[1]{0:T(128)} %bitcast.39, f32[1]{0:T(128)} %bitcast.38, f32[1]{0:T(128)} %bitcast.37), channel_id=1, replica_groups=mesh['nodes'=32,'cores'=4] {'nodes','cores'}, use_global_device_ids=true, to_apply=%region_26.27 | all-reduce | flops 3 | bytes 24 | tf_op jit(solution)/shard_map/psum | solution.py:122
  587.1 2.4 maximum_multiply_fusion
  (70 shorter events, 15.8 us)
Async XLA Ops:
  0.6 58.7 %copy-start = (f32[768,384]{1,0:T(8,128)S(1)}, f32[768,384]{1,0:T(8,128)}, u32[]{:S(2)}) copy-start(f32[768,384]{1,0:T(8,128)} %param.12) | copy-start | bytes 3538948
  24.7 1.0 copy-start.3
  37.4 0.7 copy-start.2
  47.8 23.5 %all-to-all-start = ((f32[128,2,8]{2,1,0:T(2,128)}), f32[128,2,8]{2,1,0:T(2,128)S(1)}, u32[]{:S(2)}, u32[]{:S(2)}) async-start(f32[128,2,8]{2,1,0:T(2,128)} %broadcast_select_fusion.1), calls=%async_computation | async-start | bytes 262144 | tf_op jit(solution)/shard_map/all_to_all | solution.py:81
  71.3 21.0 %copy-start.5 = (s32[3,192]{1,0:T(4,128)S(1)}, s32[3,192]{1,0:T(4,128)}, u32[]{:S(2)}) copy-start(s32[3,192]{1,0:T(4,128)} %param.17) | copy-start | bytes 6916
  71.3 52.3 %all-to-all-start.1 = ((f32[128,2,8,384]{3,2,1,0:T(8,128)}), f32[128,2,8,384]{3,2,1,0:T(8,128)}, u32[]{:S(2)}, u32[]{:S(2)}) async-start(f32[128,2,8,384]{3,2,1,0:T(8,128)} %broadcast_select_fusion), calls=%async_computation.1 | async-start | bytes 6291456 | tf_op jit(solution)/shard_map/all_to_all | solution.py:80
  168.0 5.9 copy-start.4
  464.0 125.6 %copy-start.1 = (f32[768,384]{1,0:T(8,128)S(1)}, f32[768,384]{1,0:T(8,128)}, u32[]{:S(2)}) copy-start(f32[768,384]{1,0:T(8,128)} %param.12) | copy-start | bytes 3538948
where the time goes:
time: 596 us; the launch traced here: 590 us
  blocking collectives  244 us (41%)
  local copies, waits for them, and re-layouts  150 us (25%)
  matrix products  64.4 us (11%)
  other arithmetic  59.4 us (10%)
  waiting for transfers between devices  27.9 us (5%)
  starting transfers between devices  22.1 us (4%)
  between operations  19.7 us (3%)
    psum x1, blocking collectives, on_device(): totals.append(lax.psum(local_value, ('nodes', 'cores')))  118 us
    dot_general x3, matrix products, square_step(): jnp.dot(matrix, matrix, precision=lax.Precision.HIGHEST, preferred_elemen...  64.4 us
    pmax x1, blocking collectives, on_device(): spectrum_top = lax.pmax(local_high, ('nodes', 'cores'))  62.6 us
    pmin x1, blocking collectives, on_device(): spectrum_bottom = lax.pmin(local_low, ('nodes', 'cores'))  62.6 us
    slice x4, local copies, waits for them, and re-layouts, assemble(): padded.reshape(-1)[:window_size * window_size]  27.9 us
    all_to_all x1, waiting for transfers between devices, on_device(): lax.all_to_all(outgoing, ('nodes', 'cores'), split_axis=0, concat_axis=0,...  27.9 us
    concatenate x2, local copies, waits for them, and re-layouts, assemble(): jnp.concatenate([jnp.zeros((window_size, 1), jnp.float32), near_rows, jnp...  25 us
    gather x5, local copies, waits for them, and re-layouts, on_device(): wanted = jnp.take_along_axis(slot_windows, positions, axis=1)  17 us
  transfers between devices with their start and end apart: 2, of which 1 were waited for; matrix products, arithmetic and copies ran while one was open for 3% of the time, Pallas kernels for 0%

commit v1 on v0

v1 whole, which is shorter than its diff:
```python
import jax
import jax.numpy as jnp
from jax import lax
from jax.experimental import pallas as pl
from jax.experimental.pallas import tpu as pltpu
from jax.sharding import PartitionSpec as P

CORE = 512
HALO = 256
W = 384
ITERS = 3
M = 1024
NSUB = 192
N_ORB = 98304
ORB_DEV = 768
DEVICES = 128
PER_OWNER = 8
UNITS = 21
MESSAGE = 2 * UNITS + 1
FIRST_UNIT = (0, 8, 15)
BLOCK = 256
GRID = M // BLOCK
UPPER = [(i, j) for j in range(GRID) for i in range(j + 1)]
SLOT_LANES = 16
AXES = ("nodes", "cores")
CHUNKS = 8
PACK_VMEM = 58 * 2**20
POWERS_VMEM = 24 * 2**20
FINISH_VMEM = 18 * 2**20

decay_length = 256.0
epsilon = 1e-06

F32 = jnp.float32
BF16 = jnp.bfloat16


def upper_index(i, j):
    return j * (j + 1) // 2 + i


def split3(x):
    a = x.astype(BF16)
    r = x - a.astype(F32)
    b = r.astype(BF16)
    c = (r - b.astype(F32)).astype(BF16)
    return a, b, c


def split2(x):
    a = x.astype(BF16)
    return a, (x - a.astype(F32)).astype(BF16)


def dot(a, b):
    return jnp.dot(a, b, preferred_element_type=F32)


def dot3(ah, al, bh, bl):
    return dot(jnp.concatenate([ah, ah, al], axis=1), jnp.concatenate([bh, bl, bh], axis=0))


def dot_diagonal(ah, bh, bl):
    cross = dot(ah, bl)
    return dot(ah, bh) + (cross + cross.T)


def span(first, last):
    return slice(first * BLOCK, (last + 1) * BLOCK)


def pick_rows(onehot, x):
    y = dot(onehot, jnp.concatenate(split2(x), axis=1))
    return y[:, 0:128] + y[:, 128:256]


def pick_rows_exact(onehot, x):
    a, b, c = split3(x)
    return dot(onehot, a) + dot(onehot, b) + dot(onehot, c)


def pack_kernel(dev_ref, host_ref, subs_hbm, rows_hbm, coup_hbm, ons_ref, out_ref, meta_ref,
                start_ref, rows_ref, coup_ref, held_ref, send_ref, count_ref, table_ref, sems, out_sems):
    load_subs = pltpu.make_async_copy(subs_hbm.at[:, pl.ds(0, 128)], start_ref, sems.at[0])
    load_rows = pltpu.make_async_copy(rows_hbm, rows_ref, sems.at[1])
    load_coup = pltpu.make_async_copy(coup_hbm, coup_ref, sems.at[2])
    load_rows.start()
    load_subs.start()
    load_coup.start()
    dev = dev_ref[0]

    @pl.loop(0, DEVICES, unroll=8)
    def _(h):
        count_ref[h] = 0
        table_ref[2 * h + 1] = 0

    @pl.loop(0, NSUB, unroll=8)
    def _(s):
        h = host_ref[s]
        k = count_ref[h]
        count_ref[h] = k + 1
        table_ref[2 * h + k] = s

    load_rows.wait()
    rel = rows_ref[...] - dev * ORB_DEV
    mine = (rel >= 0) & (rel < ORB_DEV)
    relf = jnp.where(mine, rel.astype(F32), 0.0)
    local = jnp.sum(relf, axis=1, keepdims=True)
    lane = lax.broadcasted_iota(jnp.int32, (8, DEVICES), 1)
    residue = (jnp.sum(jnp.where(mine[0:8], lane.astype(F32), 0.0)) * 0.125).astype(jnp.int32)
    slot_lane = lax.broadcasted_iota(jnp.int32, (ORB_DEV, ORB_DEV), 1)
    pick = slot_lane == local.astype(jnp.int32)
    onehot = jnp.where(pick, 1.0, 0.0).astype(BF16)
    onsite = jnp.concatenate([ons_ref[q:q + 1, :] for q in range(ORB_DEV // 128)], axis=1)
    energy = jnp.sum(jnp.where(pick, onsite, 0.0), axis=1, keepdims=True)
    distance = lax.broadcasted_iota(jnp.int32, (1, W), 1) + 1
    falloff = jnp.exp(-distance.astype(F32) / decay_length)
    load_coup.wait()
    for c in range(3):
        cols = slice(c * 128, (c + 1) * 128)
        parts = coup_ref[:, cols]
        for r in range(0, ORB_DEV, BLOCK):
            part = pick_rows(onehot[r:r + BLOCK], parts) * falloff[:, cols]
            held_ref[c, r:r + BLOCK, :] = part
            if r == 0:
                held_ref[c, ORB_DEV:ORB_DEV + 8, :] = part[0:8]
    lanes = lax.broadcasted_iota(jnp.int32, (ORB_DEV, 128), 1)
    diag = jnp.broadcast_to(energy, (ORB_DEV, 128))
    for t in (1, 2, 4):
        diag = jnp.where((lanes & t) == 0, diag, pltpu.roll(diag, ORB_DEV - t, 0))
    held_ref[3, 0:ORB_DEV, :] = diag
    held_ref[3, ORB_DEV:ORB_DEV + 8, :] = diag[0:8]

    load_subs.wait()
    used = jnp.where(count_ref[dev] > 1, 1, 0)
    first_sub = table_ref[2 * dev]
    second_sub = jnp.where(used == 1, table_ref[2 * dev + 1], first_sub)
    meta_ref[0] = start_ref[first_sub, 0]
    meta_ref[1] = start_ref[second_sub, 0]
    meta_ref[2] = used
    meta_ref[3] = first_sub
    meta_ref[4] = second_sub
    meta_ref[5] = dev

    lane1 = lax.broadcasted_iota(jnp.int32, (1, 128), 1)
    chunk = DEVICES // CHUNKS
    copies = []
    for q in range(CHUNKS):

        @pl.loop(q * chunk, (q + 1) * chunk, unroll=4)
        def _(h):
            energies = []
            for k in range(2):
                first = lax.shift_right_arithmetic(start_ref[table_ref[2 * h + k], 0] - residue + 127, 7)
                first = jnp.where(first >= ORB_DEV, first - ORB_DEV, first)
                for c in range(3):
                    at = h * MESSAGE + k * UNITS + FIRST_UNIT[c]
                    send_ref[pl.ds(at, 8), :] = held_ref[c, pl.ds(first, 8), :]
                energies.append(held_ref[3, pl.ds(first, 1), :])
            send_ref[pl.ds(h * MESSAGE + 2 * UNITS, 1), :] = jnp.where(lane1 < 8, energies[0], energies[1])

        part = pl.ds(q * chunk * MESSAGE, chunk * MESSAGE)
        copies.append(pltpu.make_async_copy(send_ref.at[part], out_ref.at[part], out_sems.at[q]))
        copies[-1].start()
    for copy in copies:
        copy.wait()


def pack(dev, sub_host, sub_rows, rows2d, coupling, onsite2d):
    smem = pl.BlockSpec(memory_space=pltpu.SMEM)
    vmem = pl.BlockSpec(memory_space=pltpu.VMEM)
    hbm = pl.BlockSpec(memory_space=pl.ANY)
    return pl.pallas_call(
        pack_kernel,
        out_shape=(
            jax.ShapeDtypeStruct((DEVICES * MESSAGE, 128), F32),
            jax.ShapeDtypeStruct((16,), jnp.int32),
        ),
        in_specs=[smem, smem, hbm, hbm, hbm, vmem],
        out_specs=(hbm, smem),
        scratch_shapes=[
            pltpu.SMEM((NSUB, 128), jnp.int32),
            pltpu.VMEM((ORB_DEV, DEVICES), jnp.int32),
            pltpu.VMEM((ORB_DEV, W), F32),
            pltpu.VMEM((4, ORB_DEV + 16, 128), F32),
            pltpu.VMEM((DEVICES * MESSAGE + 8, 128), F32),
            pltpu.SMEM((DEVICES,), jnp.int32),
            pltpu.SMEM((2 * DEVICES,), jnp.int32),
            pltpu.SemaphoreType.DMA((3,)),
            pltpu.SemaphoreType.DMA((CHUNKS,)),
        ],
        compiler_params=pltpu.CompilerParams(vmem_limit_bytes=PACK_VMEM),
        name="pack",
    )(dev, sub_host, sub_rows, rows2d, coupling, onsite2d)


def store_both(hi_ref, lo_ref, i, j, size, block):
    hi, lo = split2(block)
    hi_ref[i * size:(i + 1) * size, j * size:(j + 1) * size] = hi
    lo_ref[i * size:(i + 1) * size, j * size:(j + 1) * size] = lo


def build_powers(out, slot, meta_ref, branch_ref, rows_ref, got_ref, pw_ref, hh, hl, gh, gl):
    start = meta_ref[slot]
    owner = ((rows_ref[0:8].astype(F32) + 0.5) * (1.0 / ORB_DEV)).astype(jnp.int32)
    shift = lax.rem(DEVICES - lax.rem(start, DEVICES), DEVICES)
    owner = pltpu.roll(owner, shift, 1)[0:1]
    source = lax.broadcasted_iota(jnp.int32, (DEVICES, DEVICES), 0)
    onehot = jnp.where(source == owner, 1.0, 0.0).T.astype(BF16)

    def received(unit):
        return got_ref[pl.ds(unit, DEVICES, stride=MESSAGE), :]

    energies = pick_rows_exact(onehot, received(2 * UNITS)).T[8 * slot:8 * slot + 8]
    center = 0.5 * (jnp.max(energies) + jnp.min(energies))
    row = lax.broadcasted_iota(jnp.int32, (128, 128), 0)
    col = lax.broadcasted_iota(jnp.int32, (128, 128), 1)
    zero = jnp.zeros((128, 128), F32)
    for bi, bj in ((0, 5), (2, 7)):
        pw_ref[0, upper_index(bi // 2, bj // 2), 0:128, 128:256] = zero
    square_sums = [jnp.zeros((1, 128), F32) for _ in range(8)]

    def put(bi, bj, block):
        i, j = bi // 2, bj // 2
        if i <= j:
            ri, rj = (bi % 2) * 128, (bj % 2) * 128
            pw_ref[0, upper_index(i, j), ri:ri + 128, rj:rj + 128] = block
        store_both(hh, hl, bi, bj, 128, block)

    for t in range(8):
        count = min(3, 8 - t)
        near = [pick_rows(onehot, received(slot * UNITS + FIRST_UNIT[c] + t)) for c in range(count)]
        skewed = pltpu.roll(jnp.concatenate(near + [zero], axis=1), 1, 1, stride=1, stride_axis=0)
        for k in range(count + 1):
            if t + k > 7:
                continue
            upper = skewed[:, k * 128:(k + 1) * 128]
            lower = upper.T
            if k == 0:
                both = upper + lower
                square_sums[t] += jnp.sum(both * both, axis=0, keepdims=True)
                put(t, t, both + jnp.where(row == col, energies[t:t + 1] - center, 0.0))
            else:
                square_sums[t + k] += jnp.sum(upper * upper, axis=0, keepdims=True)
                square_sums[t] += jnp.sum(lower * lower, axis=0, keepdims=True)
                put(t, t + k, upper)
                put(t + k, t, lower)
        if t < 4:
            put(t, t + 4, zero)
            put(t + 4, t, zero)
        yield
    radius = 2.0 * jnp.sqrt(jnp.concatenate(square_sums, axis=0) + epsilon)
    top = jnp.max(energies + radius)
    low = jnp.max(radius - energies)

    weights = {(0, 1): 1.0, (0, 2): 1.0, (1, 1): 1.0, (1, 2): 2.0, (1, 3): 1.0, (2, 2): 1.0, (2, 3): 1.0}
    sums = [jnp.zeros((1, BLOCK), F32) for _ in range(9)]

    def add_moment(k, i, j, a, b):
        if (i, j) in weights:
            part = jnp.sum(a * b, axis=0, keepdims=True)
            sums[k] = sums[k] + (part if weights[i, j] == 1.0 else weights[i, j] * part)

    eye = lax.broadcasted_iota(jnp.int32, (BLOCK, BLOCK), 0) == lax.broadcasted_iota(jnp.int32, (BLOCK, BLOCK), 1)

    def keep(p, i, j, block, moments):
        at = upper_index(i, j)
        pw_ref[p, at] = block
        if i == j and (i, j) in weights:
            sums[p + 1] = sums[p + 1] + jnp.sum(jnp.where(eye, block, 0.0), axis=0, keepdims=True)
        for q in moments:
            add_moment(p + q + 2, i, j, block, block if p == q else pw_ref[q, at])

    def square():
        for j in range(GRID):
            for i in range(j + 1):
                mid = slice(max(0, j * BLOCK - W), min(M, (i + 1) * BLOCK + W))
                rows, cols = span(i, i), span(j, j)
                if i == j:
                    block = dot_diagonal(hh[rows, mid], hh[mid, cols], hl[mid, cols])
                else:
                    block = dot3(hh[rows, mid], hl[rows, mid], hh[mid, cols], hl[mid, cols])
                keep(1, i, j, block, ())
                store_both(gh, gl, i, j, BLOCK, block)
                if i != j:
                    store_both(gh, gl, j, i, BLOCK, block.T)
            yield

    def product(p, bh, bl, banded, moments):
        for j in range(GRID):
            mid, cols = slice(0, M), span(j, j)
            if banded:
                mid = slice(max(0, j * BLOCK - W), min(M, (j + 1) * BLOCK + W))
            for i in range(j + 1):
                rows = span(i, i)
                if banded and i == 0:
                    near = slice(0, BLOCK + W)
                    block = dot3(bh[rows, near], bl[rows, near], gh[near, cols], gl[near, cols])
                elif i == j and not banded:
                    block = dot_diagonal(gh[rows, mid], bh[mid, cols], bl[mid, cols])
                else:
                    block = dot3(gh[rows, mid], gl[rows, mid], bh[mid, cols], bl[mid, cols])
                keep(p, i, j, block, moments)
            yield

    yield from square()
    yield from product(2, hh, hl, True, (1, 2))
    yield from product(3, gh, gl, False, (2, 3))
    values = [jnp.asarray(float(CORE), F32), jnp.sum(energies[2:6] - center)]
    values += [jnp.sum(s) for s in sums[2:]]
    values += [center] + [branch_ref[t, meta_ref[3 + slot]].astype(F32) for t in range(ITERS)] + [top, low]
    lane = lax.broadcasted_iota(jnp.int32, (8, 128), 1)
    stats = jnp.zeros((8, 128), F32)
    for k, value in enumerate(values):
        stats = jnp.where(lane == slot * SLOT_LANES + k, value, stats)
    out.append(stats)


def powers_kernel(meta_ref, branch_ref, rows_ref, got_ref, pw0, pw1, send_ref, *parts):
    lane = lax.broadcasted_iota(jnp.int32, (8, 128), 1)
    empty = (lane == SLOT_LANES + 13) | (lane == SLOT_LANES + 14)
    first, second = [], []
    steps = [
        build_powers(out, k, meta_ref, branch_ref, rows_ref, got_ref, (pw0, pw1)[k], *parts[4 * k:4 * k + 4])
        for k, out in enumerate((first, second))
    ]
    for _ in range(8):
        next(steps[0])
    for _ in range(8):
        next(steps[0])
        next(steps[1])
    for step in steps:
        for _ in step:
            pass
    first, second = first[0], second[0]
    second = jnp.where(meta_ref[2] == 1, second, jnp.where(empty, -1e30, 0.0))
    send_ref[...] = jnp.broadcast_to((first + second)[0:1], (DEVICES, 128))


def powers(meta, branches, rows2d, got):
    smem = pl.BlockSpec(memory_space=pltpu.SMEM)
    vmem = pl.BlockSpec(memory_space=pltpu.VMEM)
    return pl.pallas_call(
        powers_kernel,
        out_shape=(
            jax.ShapeDtypeStruct((4, len(UPPER), BLOCK, BLOCK), F32),
            jax.ShapeDtypeStruct((4, len(UPPER), BLOCK, BLOCK), F32),
            jax.ShapeDtypeStruct((DEVICES, 128), F32),
        ),
        in_specs=[smem, smem, vmem, vmem],
        out_specs=(vmem, vmem, vmem),
        scratch_shapes=[pltpu.VMEM((M, M), BF16)] * 8,
        compiler_params=pltpu.CompilerParams(vmem_limit_bytes=POWERS_VMEM),
        name="powers",
    )(meta, branches, rows2d, got)


def purify(poly, branch):
    squared = [None] * (2 * len(poly) - 1)
    for a, pa in enumerate(poly):
        for b in range(a, len(poly)):
            term = pa * poly[b] if a == b else 2.0 * pa * poly[b]
            squared[a + b] = term if squared[a + b] is None else squared[a + b] + term
    other = [2.0 * poly[k] - value if k < len(poly) else -value for k, value in enumerate(squared)]
    return [jnp.where(branch == 0, value, out) for value, out in zip(squared, other)]


def finish_kernel(meta_ref, branch_ref, recv_ref, pw0, pw1, core_ref, occ_ref, xh0, xl0, xh1, xl1, out_ref, out_sems):
    used = meta_ref[2]
    dev = meta_ref[5]
    lane = lax.broadcasted_iota(jnp.int32, (1, 128), 1)
    most = jnp.max(recv_ref[...], axis=0, keepdims=True)
    top = jnp.max(jnp.where((lane == 13) | (lane == SLOT_LANES + 13), most, -1e30))
    low = jnp.max(jnp.where((lane == 14) | (lane == SLOT_LANES + 14), most, -1e30))
    own = recv_ref[pl.ds(dev, 1), :]
    scale = 1.0 / jnp.broadcast_to(top + low, (1, BLOCK))
    coefs = []
    for slot in range(2):
        center = jnp.sum(jnp.where(lane == SLOT_LANES * slot + 9, own, 0.0))
        poly = [(top - center) * scale, -scale]
        for t in range(2):
            poly = purify(poly, branch_ref[t, meta_ref[3 + slot]])
        coefs.append(poly)

    def occupation():
        table = recv_ref[...].T
        totals = [jnp.zeros((1, 128), F32) for _ in range(ITERS)]
        for slot in range(2):
            base = SLOT_LANES * slot
            poly = [(top - table[base + 9:base + 10]) * scale[:, 0:128], -scale[:, 0:128]]
            for t in range(ITERS):
                poly = purify(poly, table[base + 10 + t:base + 11 + t])
                for k, value in enumerate(poly):
                    totals[t] = totals[t] + value * table[base + k:base + k + 1]
        for t in range(ITERS):
            occ_ref[t] = jnp.sum(totals[t]) * (1.0 / N_ORB)

    row = lax.broadcasted_iota(jnp.int32, (BLOCK, BLOCK), 0)
    col = lax.broadcasted_iota(jnp.int32, (BLOCK, BLOCK), 1)

    def store(slot, j):
        cols = pl.ds(j * BLOCK, BLOCK)
        return pltpu.make_async_copy(
            out_ref.at[slot, :, cols], core_ref.at[slot, :, cols], out_sems.at[slot, j]
        )

    def form(slot):
        c = coefs[slot]
        pw_ref = (pw0, pw1)[slot]
        xh, xl = ((xh0, xl0), (xh1, xl1))[slot]
        constant = jnp.where(row == col, c[0], 0.0)
        for i, j in UPPER:
            at = upper_index(i, j)
            block = c[2] * pw_ref[1, at]
            for p in range(0 if j - i < GRID - 1 else 2, 4):
                if p != 1:
                    block = block + c[p + 1] * pw_ref[p, at]
            if i == j:
                block = block + constant
            hi, lo = split2(block)
            xh[span(i, i), span(j, j)] = hi
            xl[span(i, i), span(j, j)] = lo
            if i != j:
                xh[span(j, j), span(i, i)] = hi.T
                xl[span(j, j), span(i, i)] = lo.T
            yield

    def last_square(slot):
        xh, xl = ((xh0, xl0), (xh1, xl1))[slot]
        branch = branch_ref[ITERS - 1, meta_ref[3 + slot]]

        def put(i, j, acc):
            rows, cols = span(i, i), span(j, j)
            x = xh[rows, cols].astype(F32) + xl[rows, cols].astype(F32)
            value = jnp.where(branch == 0, acc, 2.0 * x - acc)
            out_ref[slot, span(i - 1, i - 1), cols] = value if slot == 0 else jnp.where(used == 1, value, 0.0)

        for j in (0, 2, 1, 3):
            cols = span(j, j)
            for i in (1, 2):
                rows = span(i, i)
                if (i, j) == (2, 1):
                    continue
                if i == j:
                    put(i, j, dot_diagonal(xh[rows, :], xh[:, cols], xl[:, cols]))
                    continue
                acc = dot3(xh[rows, :], xl[rows, :], xh[:, cols], xl[:, cols])
                put(i, j, acc)
                if (i, j) == (1, 2):
                    put(2, 1, acc.T)
            store(slot, j).start()
            yield

    for _ in form(0):
        pass
    occupation()
    forming = form(1)
    for _ in last_square(0):
        for _ in range(3):
            next(forming, None)
    for _ in last_square(1):
        pass
    for slot in range(2):
        for j in range(GRID):
            store(slot, j).wait()


def finish(meta, branches, recv, pw0, pw1):
    smem = pl.BlockSpec(memory_space=pltpu.SMEM)
    vmem = pl.BlockSpec(memory_space=pltpu.VMEM)
    hbm = pl.BlockSpec(memory_space=pl.ANY)
    return pl.pallas_call(
        finish_kernel,
        out_shape=(
            jax.ShapeDtypeStruct((2, CORE, M), F32),
            jax.ShapeDtypeStruct((ITERS,), F32),
        ),
        in_specs=[smem, smem, vmem, vmem, vmem],
        out_specs=(hbm, smem),
        scratch_shapes=[
            pltpu.VMEM((M, M), BF16),
            pltpu.VMEM((M, M), BF16),
            pltpu.VMEM((M, M), BF16),
            pltpu.VMEM((M, M), BF16),
            pltpu.VMEM((2, CORE, M), F32),
            pltpu.SemaphoreType.DMA((2, GRID)),
        ],
        compiler_params=pltpu.CompilerParams(vmem_limit_bytes=FINISH_VMEM),
        name="finish",
    )(meta, branches, recv, pw0, pw1)


def exchange(x):
    rows, lanes = x.shape
    blocks = x.reshape(DEVICES, 1, rows // DEVICES * lanes)
    return lax.all_to_all(blocks, AXES, split_axis=0, concat_axis=0, tiled=True).reshape(rows, lanes)


def on_device(coupling, onsite, row_slot, sub_rows, sub_host, branches):
    dev = lax.axis_index(AXES).astype(jnp.int32).reshape(1)
    rows2d = row_slot.reshape(ORB_DEV, DEVICES)
    send, meta = pack(dev, sub_host, sub_rows, rows2d, coupling, onsite.reshape(ORB_DEV // 128, 128))
    pw0, pw1, stats = powers(meta, branches, rows2d, exchange(send))
    return finish(meta, branches, exchange(stats), pw0, pw1)


def solution(mesh):
    return jax.shard_map(
        on_device,
        mesh=mesh,
        in_specs=(P(AXES, None), P(AXES), P(), P(), P(), P()),
        out_specs=(P(AXES, None, None), P()),
        check_vma=False,
    )
```

time: 596 us -> 102 us (0.17)
  blocking collectives: 244 us -> 63.3 us
  local copies, waits for them, and re-layouts: 150 us -> 0.01 us
  matrix products: 64.4 us -> 0 us
  other arithmetic: 59.4 us -> 0 us
  Pallas kernels: 0 us -> 37.1 us
  waiting for transfers between devices: 27.9 us -> 0 us
  starting transfers between devices: 22.1 us -> 0 us
  between operations: 19.7 us -> 0.88 us
    psum x1 -> x0, blocking collectives: 118 us -> none  [on_device(): totals.append(lax.psum(local_value, ('nodes', 'cores')))]
    dot_general x3 -> x0, matrix products: 64.4 us -> none  [square_step(): jnp.dot(matrix, matrix, precision=lax.Precision.HIGHEST, preferred_elemen...]
    all_to_all x0 -> x2, blocking collectives: none -> 63.3 us  [exchange(): lax.all_to_all(blocks, AXES, split_axis=0, concat_axis=0, tiled=True)]
    pmax x1 -> x0, blocking collectives: 62.6 us -> none  [on_device(): spectrum_top = lax.pmax(local_high, ('nodes', 'cores'))]
    pmin x1 -> x0, blocking collectives: 62.6 us -> none  [on_device(): spectrum_bottom = lax.pmin(local_low, ('nodes', 'cores'))]
    gather x16 -> x0, local copies, waits for them, and re-layouts: 56.7 us -> none  [the longest x5 17 us: on_device(): wanted = jnp.take_along_axis(slot_windows, positions, axis=1)]
    pallas_call x0 -> x3, Pallas kernels: none -> 37.1 us  [the longest x1 21.9 us: powers(): pl.pallas_call(powers_kernel, out_shape=(jax.ShapeDtypeStruct((4, len(UPP...]
    slice x6 -> x0, local copies, waits for them, and re-layouts: 29.3 us -> none  [the longest x4 27.9 us: assemble(): padded.reshape(-1)[:window_size * window_size]]
  transfers between devices with their start and end apart: 2 -> 0, of which waited for: 1 -> 0; matrix products, arithmetic and copies ran while one was open for 3% -> 0% of each run, Pallas kernels for 0% -> 0%
where the time goes in v1:
time: 102 us; the launch traced here: 101 us
  blocking collectives  63.3 us (62%)
  Pallas kernels  37.1 us (36%)
    all_to_all x2, blocking collectives, exchange(): lax.all_to_all(blocks, AXES, split_axis=0, concat_axis=0, tiled=True)  63.3 us
    pallas_call x1, Pallas kernels, powers(): pl.pallas_call(powers_kernel, out_shape=(jax.ShapeDtypeStruct((4, len(UPP...  21.9 us
    pallas_call x1, Pallas kernels, finish(): pl.pallas_call(finish_kernel, out_shape=(jax.ShapeDtypeStruct((2, CORE, M...  8.84 us
    pallas_call x1, Pallas kernels, pack(): pl.pallas_call(pack_kernel, out_shape=(jax.ShapeDtypeStruct((DEVICES * ME...  6.37 us

profile of v1, /device:TPU:1, one launch (start us, length us, event | category | flops | bytes accessed | tf_op | source)
XLA Modules:
  0.0 101.3 jit_solution(12329271698332614884)
XLA Ops:
  0.6 0.0 copy-start
  0.6 0.0 copy-start.1
  0.7 6.4 %pack.1 = (f32[5504,128]{1,0:T(8,128)}, s32[16]{0:T(128)}) custom-call(s32[1]{0:T(128)} %bitcast.dev_ref, s32[192]{0:T(256)} %host_ref.1, s32[192,1024]{1,0:T(8,128)} %subs_hbm.1, s32[768,128]{1,0:T(8,128)} %bitcast.10, f32[768,384]{1,0:T(8,128)} %coup_hbm.1, f32[6,128]{1,0:T(8,128)} %bitcast.15), custom_call_target="tpu_custom_call" | custom-call | tf_op jit(solution)/shard_map/pack/pallas_call | solution.py:173
  7.0 0.0 copy-start.2
  7.0 50.2 %all_to_all.10 = f32[128,1,5504]{2,1,0:T(1,128)S(1)} all-to-all(f32[128,1,5504]{2,1,0:T(1,128)} %bitcast.14), channel_id=1, replica_groups=mesh['nodes'=32,'cores'=4] {'nodes','cores'}, dimensions={0} | all-to-all | bytes 5636096 | tf_op jit(solution)/shard_map/all_to_all | solution.py:496
  57.3 0.0 copy-done
  57.3 0.0 copy-done.1
  57.3 0.0 copy-done.2
  57.3 21.9 %powers.1 = (f32[4,10,256,256]{3,2,1,0:T(8,128)S(1)}, f32[4,10,256,256]{3,2,1,0:T(8,128)S(1)}, f32[128,128]{1,0:T(8,128)S(1)}) custom-call(s32[16]{0:T(128)S(1)} %copy-done.2, s32[3,192]{1,0:T(4,128)S(1)} %copy-done.1, s32[768,128]{1,0:T(8,128)S(1)} %bitcast.11, f32[5504,128]{1,0:T(8,128)S(1)} %bitcast.9), custom_call_target="tpu_custom_call" | custom-call | tf_op jit(solution)/shard_map/powers/pallas_call | solution.py:343
  79.2 13.1 %all_to_all.11 = f32[128,1,128]{2,1,0:T(1,128)S(1)} all-to-all(f32[128,1,128]{2,1,0:T(1,128)S(1)} %bitcast.13), channel_id=1, replica_groups=mesh['nodes'=32,'cores'=4] {'nodes','cores'}, dimensions={0} | all-to-all | bytes 131072 | tf_op jit(solution)/shard_map/all_to_all | solution.py:496
  92.3 8.8 %finish.1 = (f32[2,512,1024]{2,1,0:T(8,128)}, f32[3]{0:T(128)}) custom-call(s32[16]{0:T(128)S(1)} %copy-done.2, s32[3,192]{1,0:T(4,128)S(1)} %copy-done.1, f32[128,128]{1,0:T(8,128)S(1)} %bitcast.12, f32[4,10,256,256]{3,2,1,0:T(8,128)S(1)} %get-tuple-element.10.pw0, f32[4,10,256,256]{3,2,1,0:T(8,128)S(1)} %get-tuple-element.11.pw1), custom_call_target="tpu_custom_call" | custom-call | tf_op jit(solution)/shard_map/finish/pallas_call | solution.py:472
Async XLA Ops:
  0.6 56.6 %copy-start = (s32[98304]{0:T(1024)S(1)}, s32[98304]{0:T(1024)}, u32[]{:S(2)}) copy-start(s32[98304]{0:T(1024)} %param.8) | copy-start | bytes 1179652
  0.6 56.6 %copy-start.1 = (s32[3,192]{1,0:T(4,128)S(1)}, s32[3,192]{1,0:T(4,128)}, u32[]{:S(2)}) copy-start(s32[3,192]{1,0:T(4,128)} %branch_ref.3) | copy-start | bytes 6916
  7.0 50.2 %copy-start.2 = (s32[16]{0:T(128)S(1)}, s32[16]{0:T(128)}, u32[]{:S(2)}) copy-start(s32[16]{0:T(128)} %get-tuple-element.7.meta_ref) | copy-start | bytes 196
